TPU v7x, 32 devices: a whole 2x2x4 slice. The times are simulated.
32 devices in a mesh: groups: 2 (over x), expert: 16 (over z, y, core).
Axes of the slice: x: 2, y: 2, z: 4, core: 2. Of those that a mesh axis runs over, the one named last changes fastest.
Arguments:
- hidden_in: bfloat16 [512, 4096], P(('groups', 'expert')), parts along dimension 0, may hold values from -6 to 6
- norm_gain: float32 [4096], replicated, may hold values from 0.5 to 1.5
- router_weight: bfloat16 [4096, 4], replicated, may hold values from -0.09375 to 0.09375
- expert_ids: int32 [512, 2], P(('groups', 'expert')), parts along dimension 0, may hold values from 0 to 3, all different within a row; in each aligned block of 8 rows (0 to 7, 8 to 15, ...) at most 6 rows name the same one
- up_weight: bfloat16 [4096, 49152], P(None, 'expert'), may hold values from -0.09375 to 0.09375
- down_weight: bfloat16 [49152, 4096], P('expert'), may hold values from -0.0546875 to 0.0546875
Outputs:
- mixed_out: bfloat16 [512, 4096], P(('groups', 'expert')), parts along dimension 0
There are 2 independent parts, one for each index of `groups`. A program takes and returns all parts, laid end to end along the dimension named above; an argument that names none is the same for every part. Nothing has to cross between parts.
Inputs may be any that keep to these rules, and one draw needn't show every extreme that they name: `expert_ids`: each row names two different experts. Rows form aligned blocks of 8 rows (one micro-batch of one device); in each block no expert is named by more than 6 rows, and in some blocks one expert is named by exactly 6 rows.
All inputs are finite; a program needn't handle non-finite values.
Results may differ from a plain program's by a relative error of at most 0.0037.
Values may be sent and summed in bfloat16 or wider, within the bound.
A program may use at most 128 MiB of HBM per device.

v0:
```python
import jax
import jax.numpy as jnp
from jax import lax
from jax.sharding import PartitionSpec as P

MICRO = 2
CAP = 6


def rms_norm(hidden_in, norm_gain):
    values = hidden_in.astype(jnp.float32)
    scale = lax.rsqrt(jnp.mean(values * values, axis=1, keepdims=True) + 1e-05)
    return (values * scale * norm_gain[None, :]).astype(jnp.bfloat16)


def pair_mix(logits, expert_ids):
    labels = jnp.arange(logits.shape[1], dtype=jnp.int32)
    match = expert_ids[:, :, None] == labels[None, None, :]
    picked = jnp.sum(jnp.where(match, logits[:, None, :], 0.0), axis=2)
    return 1.0 / (1.0 + jnp.exp(picked[:, ::-1] - picked))


def slot_places(block_ids, experts, capacity):
    flat = block_ids.reshape(-1)
    labels = jnp.arange(experts, dtype=jnp.int32)
    onehot = (flat[:, None] == labels[None, :]).astype(jnp.int32)
    before = jnp.cumsum(onehot, axis=0) - onehot
    slot = jnp.sum(before * onehot, axis=1)
    return flat * capacity + slot


def per_device(hidden_in, norm_gain, router_weight, expert_ids, up_weight, down_weight):
    devices = lax.axis_size("expert")
    experts = router_weight.shape[1]
    group = devices // experts
    width = hidden_in.shape[1]
    normed = rms_norm(hidden_in, norm_gain)
    logits = jnp.dot(normed, router_weight, preferred_element_type=jnp.float32)
    mix = pair_mix(logits, expert_ids)
    block = hidden_in.shape[0] // MICRO
    places = jnp.arange(experts * CAP, dtype=jnp.int32)
    outputs = []
    for index in range(MICRO):
        lower = index * block
        upper_row = lower + block
        normed_block = normed[lower:upper_row]
        mix_block = mix[lower:upper_row]
        position = slot_places(expert_ids[lower:upper_row], experts, CAP)
        table = position[None, :] == places[:, None]
        pick_rows = jnp.any(table.reshape(experts * CAP, block, 2), axis=2).astype(jnp.bfloat16)
        buffer = jnp.dot(pick_rows, normed_block, preferred_element_type=jnp.float32).astype(
            jnp.bfloat16
        )
        buffer = buffer.reshape(experts, CAP, width)
        outgoing = jnp.repeat(buffer, group, axis=0)
        whole = lax.all_to_all(outgoing, "expert", split_axis=0, concat_axis=0, tiled=True)
        sources = whole.shape[0]
        slots = whole.shape[1]
        flat = whole.reshape(sources * slots, width)
        hidden = jax.nn.silu(jnp.dot(flat, up_weight, preferred_element_type=jnp.float32)).astype(
            jnp.bfloat16
        )
        partial_value = jnp.dot(hidden, down_weight, preferred_element_type=jnp.float32).reshape(
            sources, slots, width
        )
        returned = lax.all_to_all(partial_value, "expert", split_axis=0, concat_axis=0, tiled=True)
        results = jnp.sum(returned.reshape(experts, group, slots, width), axis=1)
        chosen = jnp.transpose(table).reshape(block, 2, experts * CAP)
        weights = jnp.sum(jnp.where(chosen, mix_block[:, :, None], 0.0), axis=1)
        combined = jnp.dot(
            weights,
            results.reshape(experts * CAP, width),
            preferred_element_type=jnp.float32,
            precision=lax.Precision.HIGHEST,
        )
        outputs.append(
            (hidden_in[lower:upper_row].astype(jnp.float32) + combined).astype(jnp.bfloat16)
        )
    return jnp.concatenate(outputs, axis=0)


def solution(mesh):
    placed = (
        P(("groups", "expert"), None),
        P(),
        P(),
        P(("groups", "expert"), None),
        P(None, "expert"),
        P("expert", None),
    )
    return jax.shard_map(
        per_device,
        mesh=mesh,
        in_specs=placed,
        out_specs=P(("groups", "expert"), None),
        check_vma=False,
    )
```

profile of v0, /device:TPU:13, one launch (start us, length us, event | category | flops | bytes accessed | tf_op | source)
XLA Modules:
  0.0 176.3 jit_solution(13665364592949847454)
XLA Ops:
  0.0 0.0 copy-start
  0.0 0.8 fusion.17
  0.8 0.1 copy.21
  0.9 0.1 eq.87
  1.0 0.1 fusion.12
  1.1 0.2 select_reduce_fusion.3
  1.3 0.1 reduce_sum.77
  1.4 0.1 copy.16
  1.5 1.1 fusion.6
  2.5 0.1 fusion.13
  2.6 1.0 fusion.8
  3.6 0.0 copy-start.3
  3.6 0.2 convolution_convert_fusion.1
  3.9 0.1 reshape.105
  4.0 1.1 broadcast_in_dim.53
  5.1 6.6 %all-to-all-start = ((bf16[16,6,4096]{2,1,0:T(8,128)(2,1)}), bf16[16,6,4096]{2,1,0:T(8,128)(2,1)S(1)}, u32[]{:S(2)}, u32[]{:S(2)}) async-start(bf16[16,6,4096]{2,1,0:T(8,128)(2,1)} %bitcast), calls=%async_computation | async-start | bytes 2097152 | tf_op jit(solution)/shard_map/all_to_all | solution.py:56
  11.6 0.1 copy.22
  11.7 0.1 eq.100
  11.8 0.1 fusion.11
  11.9 0.2 select_reduce_fusion.1
  12.1 0.1 reduce_sum.83
  12.2 0.1 copy.19
  12.3 0.1 fusion.14
  12.3 0.0 copy-done.3
  12.3 0.3 convolution_convert_fusion
  12.6 0.1 reshape.111
  12.7 23.8 %all-to-all-done = bf16[16,6,4096]{2,1,0:T(8,128)(2,1)S(1)} async-done(((bf16[16,6,4096]{2,1,0:T(8,128)(2,1)}), bf16[16,6,4096]{2,1,0:T(8,128)(2,1)S(1)}, u32[]{:S(2)}, u32[]{:S(2)}) %all-to-all-start) | async-done | bytes 786464 | tf_op jit(solution)/shard_map/all_to_all | solution.py:56
  36.5 1.1 broadcast_in_dim.55
  37.6 4.9 %all-to-all-start.2 = ((bf16[16,6,4096]{2,1,0:T(8,128)(2,1)}), bf16[16,6,4096]{2,1,0:T(8,128)(2,1)S(1)}, u32[]{:S(2)}, u32[]{:S(2)}) async-start(bf16[16,6,4096]{2,1,0:T(8,128)(2,1)} %bitcast.20), calls=%async_computation.2 | async-start | bytes 2097152 | tf_op jit(solution)/shard_map/all_to_all | solution.py:56
  42.5 0.3 reshape.107
  42.8 19.5 %fusion.2 = f32[96,4096]{1,0:T(8,128)S(1)} fusion(bf16[3072,4096]{1,0:T(8,128)(2,1)} %param.11, bf16[96,4096]{1,0:T(8,128)(2,1)S(1)} %reshape.107, bf16[4096,3072]{1,0:T(8,128)(2,1)} %param.10), kind=kOutput, calls=%fused_computation.10 | convolution fusion | flops 4833312768 | bytes 52690944 | tf_op jit(solution)/shard_map/dot_general | solution.py:63
  62.3 1.6 reshape.108
  63.9 3.5 %all-to-all-done.2 = bf16[16,6,4096]{2,1,0:T(8,128)(2,1)S(1)} async-done(((bf16[16,6,4096]{2,1,0:T(8,128)(2,1)}), bf16[16,6,4096]{2,1,0:T(8,128)(2,1)S(1)}, u32[]{:S(2)}, u32[]{:S(2)}) %all-to-all-start.2) | async-done | bytes 786464 | tf_op jit(solution)/shard_map/all_to_all | solution.py:56
  67.4 0.0 copy-start.1
  67.4 1.0 copy-done.1
  68.4 4.9 %all-to-all-start.1 = ((f32[16,6,4096]{2,1,0:T(8,128)}), f32[16,6,4096]{2,1,0:T(8,128)S(1)}, u32[]{:S(2)}, u32[]{:S(2)}) async-start(f32[16,6,4096]{2,1,0:T(8,128)} %reshape.108), calls=%async_computation.1 | async-start | bytes 4194304 | tf_op jit(solution)/shard_map/all_to_all | solution.py:66
  73.3 1.4 reshape.113
  74.8 20.7 %fusion.3 = f32[96,4096]{1,0:T(8,128)} fusion(bf16[3072,4096]{1,0:T(8,128)(2,1)} %param.11, bf16[96,4096]{1,0:T(8,128)(2,1)S(1)} %reshape.113, bf16[4096,3072]{1,0:T(8,128)(2,1)} %param.10), kind=kOutput, calls=%fused_computation.11 | convolution fusion | flops 4833312768 | bytes 52690944 | tf_op jit(solution)/shard_map/dot_general | solution.py:63
  95.5 2.7 %reshape.114 = f32[16,6,4096]{2,1,0:T(8,128)} reshape(f32[96,4096]{1,0:T(8,128)} %fusion.3) | data formatting | bytes 3145728 | tf_op jit(solution)/shard_map/reshape | solution.py:63
  98.2 0.0 copy-start.4
  98.2 0.0 copy-start.5
  98.2 22.6 %all-to-all-done.1 = f32[16,6,4096]{2,1,0:T(8,128)S(1)} async-done(((f32[16,6,4096]{2,1,0:T(8,128)}), f32[16,6,4096]{2,1,0:T(8,128)S(1)}, u32[]{:S(2)}, u32[]{:S(2)}) %all-to-all-start.1) | async-done | bytes 1572896 | tf_op jit(solution)/shard_map/all_to_all | solution.py:66
  120.7 4.9 %all-to-all-start.3 = ((f32[16,6,4096]{2,1,0:T(8,128)}), f32[16,6,4096]{2,1,0:T(8,128)}, u32[]{:S(2)}, u32[]{:S(2)}) async-start(f32[16,6,4096]{2,1,0:T(8,128)} %reshape.114), calls=%async_computation.3 | async-start | bytes 4194304 | tf_op jit(solution)/shard_map/all_to_all | solution.py:66
  125.7 0.0 copy-done
  125.7 0.0 copy-done.4
  125.7 0.1 fusion.23
  125.8 0.0 copy-done.5
  125.9 0.1 fusion.18
  126.0 0.1 select_reduce_fusion
  126.0 0.1 bitcast_reduce_fusion.1
  126.2 0.0 copy-start.2
  126.2 0.1 reshape.110
  126.3 46.9 %all-to-all-done.3 = f32[16,6,4096]{2,1,0:T(8,128)} async-done(((f32[16,6,4096]{2,1,0:T(8,128)}), f32[16,6,4096]{2,1,0:T(8,128)}, u32[]{:S(2)}, u32[]{:S(2)}) %all-to-all-start.3) | async-done | bytes 1572896 | tf_op jit(solution)/shard_map/all_to_all | solution.py:66
  173.2 1.8 %bitcast_reduce_fusion = f32[4,6,4096]{2,1,0:T(8,128)S(1)} fusion(f32[16,6,4096]{2,1,0:T(8,128)} %all-to-all-done.3), kind=kLoop, calls=%fused_computation.6 | loop fusion | flops 294912 | bytes 1966080 | tf_op jit(solution)/shard_map/reduce_sum | solution.py:67
  174.9 0.1 reshape.116
  175.0 0.0 copy-done.2
  175.0 0.3 fusion
  175.3 0.3 fusion.1
  175.7 0.7 pad_maximum_fusion
  (8 shorter events, 0.2 us)
Async XLA Ops:
  0.0 125.7 %copy-start = (bf16[4096,4]{0,1:T(4,128)(2,1)S(1)}, bf16[4096,4]{0,1:T(4,128)(2,1)}, u32[]{:S(2)}) copy-start(bf16[4096,4]{0,1:T(4,128)(2,1)} %param.8) | copy-start | bytes 98308
  3.6 8.7 %copy-start.3 = (bf16[16,4096]{1,0:T(8,128)(2,1)}, bf16[16,4096]{1,0:T(8,128)(2,1)S(1)}, u32[]{:S(2)}) copy-start(bf16[16,4096]{1,0:T(8,128)(2,1)S(1)} %fusion.8) | copy-start | bytes 393220
  5.1 31.4 %all-to-all-start = ((bf16[16,6,4096]{2,1,0:T(8,128)(2,1)}), bf16[16,6,4096]{2,1,0:T(8,128)(2,1)S(1)}, u32[]{:S(2)}, u32[]{:S(2)}) async-start(bf16[16,6,4096]{2,1,0:T(8,128)(2,1)} %bitcast), calls=%async_computation | async-start | bytes 2097152 | tf_op jit(solution)/shard_map/all_to_all | solution.py:56
  37.6 29.8 %all-to-all-start.2 = ((bf16[16,6,4096]{2,1,0:T(8,128)(2,1)}), bf16[16,6,4096]{2,1,0:T(8,128)(2,1)S(1)}, u32[]{:S(2)}, u32[]{:S(2)}) async-start(bf16[16,6,4096]{2,1,0:T(8,128)(2,1)} %bitcast.20), calls=%async_computation.2 | async-start | bytes 2097152 | tf_op jit(solution)/shard_map/all_to_all | solution.py:56
  67.4 1.0 copy-start.1
  68.4 52.4 %all-to-all-start.1 = ((f32[16,6,4096]{2,1,0:T(8,128)}), f32[16,6,4096]{2,1,0:T(8,128)S(1)}, u32[]{:S(2)}, u32[]{:S(2)}) async-start(f32[16,6,4096]{2,1,0:T(8,128)} %reshape.108), calls=%async_computation.1 | async-start | bytes 4194304 | tf_op jit(solution)/shard_map/all_to_all | solution.py:66
  98.2 27.5 %copy-start.4 = (bf16[16,4096]{1,0:T(8,128)(2,1)S(1)}, bf16[16,4096]{1,0:T(8,128)(2,1)}, u32[]{:S(2)}) copy-start(bf16[16,4096]{1,0:T(8,128)(2,1)} %copy-done.3) | copy-start | bytes 393220
  98.2 27.6 %copy-start.5 = (s32[16,2]{0,1:T(2,128)S(1)}, s32[16,2]{0,1:T(2,128)}, u32[]{:S(2)}) copy-start(s32[16,2]{0,1:T(2,128)} %param.9) | copy-start | bytes 388
  120.7 52.4 %all-to-all-start.3 = ((f32[16,6,4096]{2,1,0:T(8,128)}), f32[16,6,4096]{2,1,0:T(8,128)}, u32[]{:S(2)}, u32[]{:S(2)}) async-start(f32[16,6,4096]{2,1,0:T(8,128)} %reshape.114), calls=%async_computation.3 | async-start | bytes 4194304 | tf_op jit(solution)/shard_map/all_to_all | solution.py:66
  126.2 48.8 %copy-start.2 = (bf16[16,4096]{1,0:T(8,128)(2,1)S(1)}, bf16[16,4096]{1,0:T(8,128)(2,1)}, u32[]{:S(2)}) copy-start(bf16[16,4096]{1,0:T(8,128)(2,1)} %param.6) | copy-start | bytes 393220
where the time goes:
time: 177 us; the launch traced here: 176 us
  waiting for transfers between devices  96.8 us (55%)
  matrix products  41.5 us (23%)
  starting transfers between devices  21.3 us (12%)
  local copies, waits for them, and re-layouts  11 us (6%)
  other arithmetic  5.52 us (3%)
    all_to_all x2, waiting for transfers between devices, per_device(): lax.all_to_all(partial_value, 'expert', split_axis=0, concat_axis=0, tile...  69.5 us
    dot_general x2, matrix products, per_device(): jnp.dot(hidden, down_weight, preferred_element_type=jnp.float32)  40.2 us
    all_to_all x2, waiting for transfers between devices, per_device(): lax.all_to_all(outgoing, 'expert', split_axis=0, concat_axis=0, tiled=True)  27.3 us
    all_to_all x2, starting transfers between devices, per_device(): lax.all_to_all(outgoing, 'expert', split_axis=0, concat_axis=0, tiled=True)  11.5 us
    all_to_all x2, starting transfers between devices, per_device(): lax.all_to_all(partial_value, 'expert', split_axis=0, concat_axis=0, tile...  9.85 us
    reshape x2, local copies, waits for them, and re-layouts, per_device(): jnp.dot(hidden, down_weight, preferred_element_type=jnp.float32)  4.28 us
  transfers between devices with their start and end apart: 4, of which 4 were waited for; matrix products, arithmetic and copies ran while one was open for 27% of the time, Pallas kernels for 0%

commit v1 on v0

v1 whole, which is shorter than its diff:
```python
import functools

import jax
import jax.numpy as jnp
from jax import lax
from jax.experimental import pallas as pl
from jax.experimental.pallas import tpu as pltpu
from jax.sharding import PartitionSpec as P

MESH = pl.DeviceIdType.MESH
BF = jnp.bfloat16
F32 = jnp.float32
EXTRA = 128


def tile_of(size):
    for tile in (512, 384, 256, 128):
        if size % tile == 0:
            return tile
    return size


def kernel(
    devices, experts, hid_ref, gain_ref, router_ref, ids_ref, up_ref, down_ref, out_ref,
    rows_buf, up_buf, down_buf, hidden_buf, part, from_core, from_peer, from_plane, factor_buf,
    up_sem, down_sem, d1_send, d1_recv, d2_send, d2_recv, d3_send, d3_recv,
    r1_send, r1_recv, r2_send, r2_recv, r3_send, r3_recv,
):
    group = devices // experts
    peers = group // 2
    rows, width = hid_ref.shape
    ups, _, up_tile = up_buf.shape
    downs, _, down_tile = down_buf.shape
    half = experts * peers * rows
    span = experts * rows
    me = lax.axis_index("expert")
    plane = me // group
    peer = lax.rem(me, group) // 2
    core = lax.rem(me, 2)

    def index(p, h, c):
        return p * group + h * 2 + c

    def place(p, h, c):
        return pl.multiple_of(((c * peers + h) * experts + p) * rows, rows)

    def other_plane(step):
        return lax.rem(plane + step, experts)

    def source_plane(step):
        return lax.rem(plane + experts - step, experts)

    def other_peer(step):
        return lax.rem(peer + step, peers)

    def source_peer(step):
        return lax.rem(peer + peers - step, peers)

    def remote(src, dst, send, recv, target):
        return pltpu.make_async_remote_copy(
            src_ref=src, dst_ref=dst, send_sem=send, recv_sem=recv,
            device_id={"expert": target}, device_id_type=MESH,
        )

    def up_copy(i):
        return pltpu.make_async_copy(
            up_ref.at[:, pl.ds(pl.multiple_of(i * up_tile, up_tile), up_tile)], up_buf.at[i], up_sem.at[i]
        )

    def down_copy(i):
        return pltpu.make_async_copy(
            down_ref.at[:, pl.ds(pl.multiple_of(i * down_tile, down_tile), down_tile)],
            down_buf.at[i], down_sem.at[i],
        )

    barrier = pltpu.get_barrier_semaphore()
    friends = [index(other_plane(s), peer, core) for s in range(1, experts)]
    friends += [index(plane, other_peer(s), core) for s in range(1, peers)]
    friends += [index(plane, peer, 1 - core)]
    for friend in friends:
        pl.semaphore_signal(barrier, inc=1, device_id={"expert": friend}, device_id_type=MESH)

    for i in range(ups):
        up_copy(i).start()
    for i in range(downs):
        down_copy(i).start()

    values = hid_ref[...].astype(F32)
    scale = lax.rsqrt(jnp.mean(values * values, axis=1, keepdims=True) + 1e-05)
    normed = (values * scale * gain_ref[...]).astype(BF)
    own = pl.ds(place(plane, peer, core), rows)
    rows_buf[own, :width] = normed
    normed32 = normed.astype(F32)
    router = router_ref[...].astype(F32)
    logits = [jnp.sum(normed32 * router[e:e + 1, :], axis=1, keepdims=True) for e in range(experts)]
    first, second = ids_ref[:, 0:1], ids_ref[:, 1:2]
    picked = [
        sum(jnp.where(ids == e, logits[e], 0.0) for e in range(experts)) for ids in (first, second)
    ]
    mix0 = 1.0 / (1.0 + jnp.exp(picked[1] - picked[0]))
    mix1 = 1.0 / (1.0 + jnp.exp(picked[0] - picked[1]))
    lane = lax.broadcasted_iota(jnp.int32, (rows, EXTRA), 1)
    label = lax.rem(lane, experts)
    factor = jnp.where(first == label, mix0, 0.0) + jnp.where(second == label, mix1, 0.0)
    high = factor.astype(BF)
    low = (factor - high.astype(F32)).astype(BF)
    rows_buf[own, width:] = jnp.where(
        lane < experts, high.astype(F32), jnp.where(lane < 2 * experts, low.astype(F32), 0.0)
    ).astype(BF)

    pl.semaphore_wait(barrier, len(friends))

    def block(p, h, c):
        return rows_buf.at[pl.ds(place(p, h, c), rows)]

    def d1(step):
        b = block(plane, peer, core)
        return remote(b, b, d1_send.at[step - 1], d1_recv.at[step - 1],
                      index(other_plane(step), peer, core))

    def d2(j, step):
        b = block(source_plane(step), peer, core)
        return remote(b, b, d2_send.at[j - 1, step], d2_recv.at[j - 1, step],
                      index(plane, other_peer(j), core))

    def d3(j, step):
        b = block(source_plane(step), source_peer(j), core)
        return remote(b, b, d3_send.at[j, step], d3_recv.at[j, step],
                      index(plane, peer, 1 - core))

    for step in range(1, experts):
        d1(step).start()
    for step in range(experts):
        if step:
            d1(step).wait_recv()
        for j in range(1, peers):
            d2(j, step).start()
        d3(0, step).start()
    for step in range(experts):
        for j in range(1, peers):
            d2(j, step).wait_recv()
            d3(j, step).start()
    for step in range(experts):
        for j in range(peers):
            d3(j, step).wait_recv()

    lane_all = lax.broadcasted_iota(jnp.int32, (2 * half, EXTRA), 1)
    chosen = (lane_all == plane) | (lane_all == plane + experts)
    factor_buf[...] = jnp.broadcast_to(
        jnp.sum(jnp.where(chosen, rows_buf[:, width:].astype(F32), 0.0), axis=1, keepdims=True),
        factor_buf.shape,
    )

    @pl.loop(0, ups)
    def _(i):
        up_copy(i).wait()
        value = jnp.dot(rows_buf[:, :width], up_buf[i], preferred_element_type=F32)
        hidden_buf[:, pl.ds(pl.multiple_of(i * up_tile, up_tile), up_tile)] = (
            value / (1.0 + jnp.exp(-value))
        ).astype(BF)

    base = pl.multiple_of(core * half, rows)
    away = pl.multiple_of((1 - core) * half, rows)
    mine = pl.multiple_of(base + peer * span, rows)
    final = pl.multiple_of(mine + plane * rows, rows)

    def r1(k):
        return remote(part.at[k, pl.ds(away, half)], from_core.at[k], r1_send.at[k], r1_recv.at[k],
                      index(plane, peer, 1 - core))

    def r2(k, j):
        start = pl.multiple_of(base + other_peer(j) * span, rows)
        return remote(part.at[k, pl.ds(start, span)], from_peer.at[k, j - 1],
                      r2_send.at[k, j - 1], r2_recv.at[k, j - 1],
                      index(plane, other_peer(j), core))

    def r3(k, step):
        start = pl.multiple_of(mine + other_plane(step) * rows, rows)
        return remote(part.at[k, pl.ds(start, rows)], from_plane.at[k, step - 1],
                      r3_send.at[k, step - 1], r3_recv.at[k, step - 1],
                      index(other_plane(step), peer, core))

    @pl.loop(0, downs + 5)
    def _(i):
        @pl.when(i < downs)
        def _():
            down_copy(i).wait()
            value = jnp.dot(hidden_buf[...], down_buf[i], preferred_element_type=F32)
            part[i] = (value * factor_buf[:, 0:1]).astype(BF)
            r1(i).start()

        @pl.when((i >= 1) & (i < downs + 1))
        def _():
            k = i - 1
            r1(k).wait_recv()
            part[k, pl.ds(base, half)] = (
                part[k, pl.ds(base, half)].astype(F32) + from_core[k].astype(F32)
            ).astype(BF)
            for j in range(1, peers):
                r2(k, j).start()

        @pl.when((i >= 3) & (i < downs + 3))
        def _():
            k = i - 3
            total = part[k, pl.ds(mine, span)].astype(F32)
            for j in range(1, peers):
                r2(k, j).wait_recv()
                total = total + from_peer[k, j - 1].astype(F32)
            part[k, pl.ds(mine, span)] = total.astype(BF)
            for step in range(1, experts):
                r3(k, step).start()

        @pl.when(i >= 5)
        def _():
            k = i - 5
            cols = pl.ds(pl.multiple_of(k * down_tile, down_tile), down_tile)
            total = part[k, pl.ds(final, rows)].astype(F32)
            for step in range(1, experts):
                r3(k, step).wait_recv()
                total = total + from_plane[k, step - 1].astype(F32)
            out_ref[:, cols] = (hid_ref[:, cols].astype(F32) + total).astype(BF)

    for step in range(1, experts):
        d1(step).wait_send()
    for step in range(experts):
        for j in range(1, peers):
            d2(j, step).wait_send()
        for j in range(peers):
            d3(j, step).wait_send()

    @pl.loop(0, downs)
    def _(k):
        r1(k).wait_send()
        for j in range(1, peers):
            r2(k, j).wait_send()
        for step in range(1, experts):
            r3(k, step).wait_send()


def per_device(hidden_in, norm_gain, router_weight, expert_ids, up_weight, down_weight):
    devices = lax.axis_size("expert")
    experts = router_weight.shape[1]
    peers = devices // experts // 2
    rows, width = hidden_in.shape
    depth = up_weight.shape[1]
    up_tile, down_tile = tile_of(depth), tile_of(width)
    ups, downs = depth // up_tile, width // down_tile
    whole = devices * rows
    dma = pltpu.SemaphoreType.DMA
    vmem = pl.BlockSpec(memory_space=pltpu.VMEM)
    return pl.pallas_call(
        functools.partial(kernel, devices, experts),
        out_shape=jax.ShapeDtypeStruct((rows, width), BF),
        in_specs=[vmem] * 4 + [pl.BlockSpec(memory_space=pl.ANY)] * 2,
        out_specs=vmem,
        scratch_shapes=[
            pltpu.VMEM((whole, width + EXTRA), BF),
            pltpu.VMEM((ups, width, up_tile), BF),
            pltpu.VMEM((downs, depth, down_tile), BF),
            pltpu.VMEM((whole, depth), BF),
            pltpu.VMEM((downs, whole, down_tile), BF),
            pltpu.VMEM((downs, whole // 2, down_tile), BF),
            pltpu.VMEM((downs, max(peers - 1, 1), experts * rows, down_tile), BF),
            pltpu.VMEM((downs, experts - 1, rows, down_tile), BF),
            pltpu.VMEM((whole, 128), F32),
            dma((ups,)), dma((downs,)),
            dma((experts - 1,)), dma((experts - 1,)),
            dma((max(peers - 1, 1), experts)), dma((max(peers - 1, 1), experts)),
            dma((peers, experts)), dma((peers, experts)),
            dma((downs,)), dma((downs,)),
            dma((downs, max(peers - 1, 1))), dma((downs, max(peers - 1, 1))),
            dma((downs, experts - 1)), dma((downs, experts - 1)),
        ],
        compiler_params=pltpu.CompilerParams(
            collective_id=0, has_side_effects=True, vmem_limit_bytes=62 * 1024 * 1024
        ),
        cost_estimate=pl.CostEstimate(
            flops=4 * whole * width * depth, bytes_accessed=4 * width * depth, transcendentals=whole * depth
        ),
    )(hidden_in, norm_gain[None, :], router_weight.T, expert_ids, up_weight, down_weight)


def solution(mesh):
    placed = (
        P(("groups", "expert"), None),
        P(),
        P(),
        P(("groups", "expert"), None),
        P(None, "expert"),
        P("expert", None),
    )
    return jax.shard_map(
        per_device,
        mesh=mesh,
        in_specs=placed,
        out_specs=P(("groups", "expert"), None),
        check_vma=False,
    )
```

time: 177 us -> 60.4 us (0.34)
  the two profiles are of different devices: /device:TPU:13 before, /device:TPU:0 now
where the time goes in v1:
time: 60.4 us; the launch traced here: 60.2 us
  Pallas kernels  57.3 us (95%)
  local copies, waits for them, and re-layouts  2.92 us (5%)
    pallas_call x1, Pallas kernels, per_device(): pl.pallas_call(functools.partial(kernel, devices, experts), out_shape=jax...  57.3 us
    unnamed x2, local copies, waits for them, and re-layouts  2.92 us

profile of v1, /device:TPU:0, one launch (start us, length us, event | category | flops | bytes accessed | tf_op | source)
XLA Modules:
  0.0 60.2 jit_solution(78392954814408021)
XLA Ops:
  0.0 1.4 %copy.7.ids_ref = s32[16,2]{1,0:T(8,128)} copy(s32[16,2]{0,1:T(2,128)} %param.9) | data formatting | bytes 256 | tf_op args[3]
  1.4 57.3 %shard_map.64 = bf16[16,4096]{1,0:T(8,128)(2,1)} custom-call(bf16[16,4096]{1,0:T(8,128)(2,1)} %hid_ref.1, f32[1,4096]{1,0:T(1,128)} %bitcast.3, bf16[4,4096]{1,0:T(4,128)(2,1)} %bitcast.2, s32[16,2]{1,0:T(8,128)} %copy.7.ids_ref, bf16[4096,3072]{1,0:T(8,128)(2,1)} %up_ref.1, bf16[3072,4096]{1,0:T(8,128)(2,1)} %down_ref.1), custom_call_target="tpu_custom_call" | custom-call | flops 12884901888 | bytes 50331648 | tf_op jit(solution)/shard_map/pallas_call | solution.py:251
  58.7 1.6 %copy.9 = bf16[16,4096]{1,0:T(8,128)(2,1)} copy(bf16[16,4096]{1,0:T(8,128)(2,1)} %shard_map.64) | data formatting | bytes 262144

commit v2 on v1

--- a/solution.py
+++ b/solution.py
@@ -11,6 +11,7 @@
 BF = jnp.bfloat16
 F32 = jnp.float32
 EXTRA = 128
+CHUNKS = 4
 
 
 def tile_of(size):
@@ -22,7 +23,7 @@
 
 def kernel(
     devices, experts, hid_ref, gain_ref, router_ref, ids_ref, up_ref, down_ref, out_ref,
-    rows_buf, up_buf, down_buf, hidden_buf, part, from_core, from_peer, from_plane, factor_buf,
+    rows_buf, up_buf, down_buf, hidden_buf, part, from_core, from_peer, from_plane, factor_buf, sums,
     up_sem, down_sem, d1_send, d1_recv, d2_send, d2_recv, d3_send, d3_recv,
     r1_send, r1_recv, r2_send, r2_recv, r3_send, r3_recv,
 ):
@@ -93,7 +94,13 @@
     normed32 = normed.astype(F32)
     router = router_ref[...].astype(F32)
     logits = [jnp.sum(normed32 * router[e:e + 1, :], axis=1, keepdims=True) for e in range(experts)]
-    first, second = ids_ref[:, 0:1], ids_ref[:, 1:2]
+    square = (rows, rows)
+    eye = lax.broadcasted_iota(jnp.int32, square, 0) == lax.broadcasted_iota(jnp.int32, square, 1)
+    ids_rows = ids_ref[...].astype(F32)
+    first, second = [
+        jnp.sum(jnp.where(eye, ids_rows[k:k + 1, :], 0.0), axis=1, keepdims=True).astype(jnp.int32)
+        for k in range(2)
+    ]
     picked = [
         sum(jnp.where(ids == e, logits[e], 0.0) for e in range(experts)) for ids in (first, second)
     ]
@@ -110,39 +117,72 @@
 
     pl.semaphore_wait(barrier, len(friends))
 
-    def block(p, h, c):
-        return rows_buf.at[pl.ds(place(p, h, c), rows)]
-
-    def d1(step):
-        b = block(plane, peer, core)
-        return remote(b, b, d1_send.at[step - 1], d1_recv.at[step - 1],
+    depth_tile = width // CHUNKS
+
+    def block(p, h, c, q):
+        cols = depth_tile + (EXTRA if q == CHUNKS - 1 else 0)
+        return rows_buf.at[pl.ds(place(p, h, c), rows), pl.ds(q * depth_tile, cols)]
+
+    def d1(q, step):
+        b = block(plane, peer, core, q)
+        return remote(b, b, d1_send.at[q, step - 1], d1_recv.at[q, step - 1],
                       index(other_plane(step), peer, core))
 
-    def d2(j, step):
-        b = block(source_plane(step), peer, core)
-        return remote(b, b, d2_send.at[j - 1, step], d2_recv.at[j - 1, step],
+    def d2(q, j, step):
+        b = block(source_plane(step), peer, core, q)
+        return remote(b, b, d2_send.at[q, j - 1, step], d2_recv.at[q, j - 1, step],
                       index(plane, other_peer(j), core))
 
-    def d3(j, step):
-        b = block(source_plane(step), source_peer(j), core)
-        return remote(b, b, d3_send.at[j, step], d3_recv.at[j, step],
+    def d3(q, j, step):
+        b = block(source_plane(step), source_peer(j), core, q)
+        return remote(b, b, d3_send.at[q, j, step], d3_recv.at[q, j, step],
                       index(plane, peer, 1 - core))
 
-    for step in range(1, experts):
-        d1(step).start()
-    for step in range(experts):
-        if step:
-            d1(step).wait_recv()
-        for j in range(1, peers):
-            d2(j, step).start()
-        d3(0, step).start()
-    for step in range(experts):
-        for j in range(1, peers):
-            d2(j, step).wait_recv()
-            d3(j, step).start()
-    for step in range(experts):
-        for j in range(peers):
-            d3(j, step).wait_recv()
+    def pass_on_planes(q):
+        for step in range(experts):
+            if step:
+                d1(q, step).wait_recv()
+            for j in range(1, peers):
+                d2(q, j, step).start()
+            d3(q, 0, step).start()
+
+    def pass_on_peers(q):
+        for step in range(experts):
+            for j in range(1, peers):
+                d2(q, j, step).wait_recv()
+                d3(q, j, step).start()
+
+    def multiply(q):
+        for step in range(experts):
+            for j in range(peers):
+                d3(q, j, step).wait_recv()
+        span_q = slice(q * depth_tile, (q + 1) * depth_tile)
+
+        @pl.loop(0, ups)
+        def _(i):
+            if q == 0:
+                up_copy(i).wait()
+            value = jnp.dot(rows_buf[:, span_q], up_buf[i, span_q, :], preferred_element_type=F32)
+            if q:
+                value = sums[i] + value
+            if q < CHUNKS - 1:
+                sums[i] = value
+            else:
+                hidden_buf[:, pl.ds(pl.multiple_of(i * up_tile, up_tile), up_tile)] = (
+                    value / (1.0 + jnp.exp(-value))
+                ).astype(BF)
+
+    for q in range(CHUNKS):
+        for step in range(1, experts):
+            d1(q, step).start()
+    pass_on_planes(0)
+    for q in range(CHUNKS):
+        if q + 1 < CHUNKS:
+            pass_on_planes(q + 1)
+        pass_on_peers(q)
+        if q:
+            multiply(q - 1)
+    multiply(CHUNKS - 1)
 
     lane_all = lax.broadcasted_iota(jnp.int32, (2 * half, EXTRA), 1)
     chosen = (lane_all == plane) | (lane_all == plane + experts)
@@ -150,14 +190,6 @@
         jnp.sum(jnp.where(chosen, rows_buf[:, width:].astype(F32), 0.0), axis=1, keepdims=True),
         factor_buf.shape,
     )
-
-    @pl.loop(0, ups)
-    def _(i):
-        up_copy(i).wait()
-        value = jnp.dot(rows_buf[:, :width], up_buf[i], preferred_element_type=F32)
-        hidden_buf[:, pl.ds(pl.multiple_of(i * up_tile, up_tile), up_tile)] = (
-            value / (1.0 + jnp.exp(-value))
-        ).astype(BF)
 
     base = pl.multiple_of(core * half, rows)
     away = pl.multiple_of((1 - core) * half, rows)
@@ -220,13 +252,14 @@
                 total = total + from_plane[k, step - 1].astype(F32)
             out_ref[:, cols] = (hid_ref[:, cols].astype(F32) + total).astype(BF)
 
-    for step in range(1, experts):
-        d1(step).wait_send()
-    for step in range(experts):
-        for j in range(1, peers):
-            d2(j, step).wait_send()
-        for j in range(peers):
-            d3(j, step).wait_send()
+    for q in range(CHUNKS):
+        for step in range(1, experts):
+            d1(q, step).wait_send()
+        for step in range(experts):
+            for j in range(1, peers):
+                d2(q, j, step).wait_send()
+            for j in range(peers):
+                d3(q, j, step).wait_send()
 
     @pl.loop(0, downs)
     def _(k):
@@ -263,21 +296,22 @@
             pltpu.VMEM((downs, max(peers - 1, 1), experts * rows, down_tile), BF),
             pltpu.VMEM((downs, experts - 1, rows, down_tile), BF),
             pltpu.VMEM((whole, 128), F32),
+            pltpu.VMEM((ups, whole, up_tile), F32),
             dma((ups,)), dma((downs,)),
-            dma((experts - 1,)), dma((experts - 1,)),
-            dma((max(peers - 1, 1), experts)), dma((max(peers - 1, 1), experts)),
-            dma((peers, experts)), dma((peers, experts)),
+            dma((CHUNKS, experts - 1)), dma((CHUNKS, experts - 1)),
+            dma((CHUNKS, max(peers - 1, 1), experts)), dma((CHUNKS, max(peers - 1, 1), experts)),
+            dma((CHUNKS, peers, experts)), dma((CHUNKS, peers, experts)),
             dma((downs,)), dma((downs,)),
             dma((downs, max(peers - 1, 1))), dma((downs, max(peers - 1, 1))),
             dma((downs, experts - 1)), dma((downs, experts - 1)),
         ],
         compiler_params=pltpu.CompilerParams(
-            collective_id=0, has_side_effects=True, vmem_limit_bytes=62 * 1024 * 1024
+            collective_id=0, has_side_effects=True, vmem_limit_bytes=63 * 1024 * 1024
         ),
         cost_estimate=pl.CostEstimate(
             flops=4 * whole * width * depth, bytes_accessed=4 * width * depth, transcendentals=whole * depth
         ),
-    )(hidden_in, norm_gain[None, :], router_weight.T, expert_ids, up_weight, down_weight)
+    )(hidden_in, norm_gain[None, :], router_weight.T, expert_ids.T, up_weight, down_weight)
 
 
 def solution(mesh):

time: 60.4 us -> 57.9 us (0.959)
  local copies, waits for them, and re-layouts: 2.92 us -> 1.57 us
  Pallas kernels: 57.3 us -> 56.2 us
    unnamed x2 -> x1, local copies, waits for them, and re-layouts: 2.92 us -> 1.57 us
    pallas_call x1, Pallas kernels: 57.3 us -> 56.2 us  [per_device(): pl.pallas_call(functools.partial(kernel, devices, experts), out_shape=jax...]
where the time goes in v2:
time: 57.9 us; the launch traced here: 57.8 us
  Pallas kernels  56.2 us (97%)
  local copies, waits for them, and re-layouts  1.57 us (3%)
    pallas_call x1, Pallas kernels, per_device(): pl.pallas_call(functools.partial(kernel, devices, experts), out_shape=jax...  56.2 us
    unnamed x1, local copies, waits for them, and re-layouts  1.57 us

profile of v2, /device:TPU:0, one launch (start us, length us, event | category | flops | bytes accessed | tf_op | source)
XLA Modules:
  0.0 57.8 jit_solution(13184398956302793141)
XLA Ops:
  0.0 56.2 %shard_map.64 = bf16[16,4096]{1,0:T(8,128)(2,1)} custom-call(bf16[16,4096]{1,0:T(8,128)(2,1)} %hid_ref.1, f32[1,4096]{1,0:T(1,128)} %bitcast.4, bf16[4,4096]{1,0:T(4,128)(2,1)} %bitcast.3, s32[2,16]{1,0:T(2,128)} %bitcast.5, bf16[4096,3072]{1,0:T(8,128)(2,1)} %up_ref.1, bf16[3072,4096]{1,0:T(8,128)(2,1)} %down_ref.1), custom_call_target="tpu_custom_call" | custom-call | flops 12884901888 | bytes 50331648 | tf_op jit(solution)/shard_map/pallas_call | solution.py:284
  56.2 1.6 %copy.8 = bf16[16,4096]{1,0:T(8,128)(2,1)} copy(bf16[16,4096]{1,0:T(8,128)(2,1)} %shard_map.64) | data formatting | bytes 262144

commit v3 on v2

--- a/solution.py
+++ b/solution.py
@@ -12,6 +12,7 @@
 F32 = jnp.float32
 EXTRA = 128
 CHUNKS = 4
+WINDOW = 2
 
 
 def tile_of(size):
@@ -145,6 +146,9 @@
             for j in range(1, peers):
                 d2(q, j, step).start()
             d3(q, 0, step).start()
+        if q + WINDOW < CHUNKS:
+            for step in range(1, experts):
+                d1(q + WINDOW, step).start()
 
     def pass_on_peers(q):
         for step in range(experts):
@@ -172,7 +176,7 @@
                     value / (1.0 + jnp.exp(-value))
                 ).astype(BF)
 
-    for q in range(CHUNKS):
+    for q in range(WINDOW):
         for step in range(1, experts):
             d1(q, step).start()
     pass_on_planes(0)
@@ -212,7 +216,7 @@
                       r3_send.at[k, step - 1], r3_recv.at[k, step - 1],
                       index(other_plane(step), peer, core))
 
-    @pl.loop(0, downs + 5)
+    @pl.loop(0, downs + 8)
     def _(i):
         @pl.when(i < downs)
         def _():
@@ -221,9 +225,9 @@
             part[i] = (value * factor_buf[:, 0:1]).astype(BF)
             r1(i).start()
 
-        @pl.when((i >= 1) & (i < downs + 1))
+        @pl.when((i >= 2) & (i < downs + 2))
         def _():
-            k = i - 1
+            k = i - 2
             r1(k).wait_recv()
             part[k, pl.ds(base, half)] = (
                 part[k, pl.ds(base, half)].astype(F32) + from_core[k].astype(F32)
@@ -231,9 +235,9 @@
             for j in range(1, peers):
                 r2(k, j).start()
 
-        @pl.when((i >= 3) & (i < downs + 3))
+        @pl.when((i >= 5) & (i < downs + 5))
         def _():
-            k = i - 3
+            k = i - 5
             total = part[k, pl.ds(mine, span)].astype(F32)
             for j in range(1, peers):
                 r2(k, j).wait_recv()
@@ -242,9 +246,9 @@
             for step in range(1, experts):
                 r3(k, step).start()
 
-        @pl.when(i >= 5)
+        @pl.when(i >= 8)
         def _():
-            k = i - 5
+            k = i - 8
             cols = pl.ds(pl.multiple_of(k * down_tile, down_tile), down_tile)
             total = part[k, pl.ds(final, rows)].astype(F32)
             for step in range(1, experts):

time: 57.9 us -> 54.8 us (0.946)
  Pallas kernels: 56.2 us -> 53.1 us
    pallas_call x1, Pallas kernels: 56.2 us -> 53.1 us  [per_device(): pl.pallas_call(functools.partial(kernel, devices, experts), out_shape=jax...]
where the time goes in v3:
time: 54.8 us; the launch traced here: 54.7 us
  Pallas kernels  53.1 us (97%)
  local copies, waits for them, and re-layouts  1.57 us (3%)
    pallas_call x1, Pallas kernels, per_device(): pl.pallas_call(functools.partial(kernel, devices, experts), out_shape=jax...  53.1 us
    unnamed x1, local copies, waits for them, and re-layouts  1.57 us

profile of v3, /device:TPU:0, one launch (start us, length us, event | category | flops | bytes accessed | tf_op | source)
XLA Modules:
  0.0 54.7 jit_solution(7216702971206949684)
XLA Ops:
  0.0 53.1 %shard_map.64 = bf16[16,4096]{1,0:T(8,128)(2,1)} custom-call(bf16[16,4096]{1,0:T(8,128)(2,1)} %hid_ref.1, f32[1,4096]{1,0:T(1,128)} %bitcast.4, bf16[4,4096]{1,0:T(4,128)(2,1)} %bitcast.3, s32[2,16]{1,0:T(2,128)} %bitcast.5, bf16[4096,3072]{1,0:T(8,128)(2,1)} %up_ref.1, bf16[3072,4096]{1,0:T(8,128)(2,1)} %down_ref.1), custom_call_target="tpu_custom_call" | custom-call | flops 12884901888 | bytes 50331648 | tf_op jit(solution)/shard_map/pallas_call | solution.py:288
  53.1 1.6 %copy.8 = bf16[16,4096]{1,0:T(8,128)(2,1)} copy(bf16[16,4096]{1,0:T(8,128)(2,1)} %shard_map.64) | data formatting | bytes 262144
